TPU v7x, 32 devices: a whole 2x2x4 slice. The times are simulated.
32 devices in a mesh: gene: 8 (over y, x, core), samp: 4 (over z).
Axes of the slice: x: 2, y: 2, z: 4, core: 2. Of those that a mesh axis runs over, the one named last changes fastest.
Arguments:
- dosage: bfloat16 [6144, 5120], P('gene', 'samp'), may hold values from 0 to 2
- expression: float32 [5120, 16], P('samp', 'gene'), may hold values from -6 to 6
- perms: int32 [128, 5120], P(None, 'samp'), may hold values from 0 to 5119, each once within a row
- windows: int32 [16, 2], P('gene'), may hold values from 0 to 6144, as said below
- order: int32 [16], replicated, may hold values from 0 to 15, each once
Outputs:
- observed: float32 [16], P('gene')
- successive: float32 [16, 128], P('gene')
Inputs may be any that keep to these rules, and one draw needn't show every extreme that they name: `windows`: gene i's window [start, end) starts within the 768 variants before the block of variants i // 2 * 768 to (i // 2 + 1) * 768 - 1, or at 0, and ends within the 768 variants after that block, or at 6144; start < end.
All inputs are finite; a program needn't handle non-finite values.
Results may differ from a plain program's by a relative error of at most 0.0015.
Values may be sent and summed in bfloat16 or wider, within the bound.
A program may use at most 128 MiB of HBM per device.

v0:
```python
import jax
import jax.numpy as jnp
from jax import lax
from jax.sharding import PartitionSpec as P

epsilon = 1e-06


def padded(block, sides, width):
    for axis, dim in sides:
        count = lax.axis_size(axis)
        forward = [(i, i + 1) for i in range(count - 1)]
        backward = [(target, source) for source, target in forward]
        low = lax.ppermute(
            lax.slice_in_dim(block, block.shape[dim] - width, None, axis=dim), axis, forward
        )
        high = lax.ppermute(lax.slice_in_dim(block, 0, width, axis=dim), axis, backward)
        block = jnp.concatenate([low, block, high], axis=dim)
    return block


def prefix(shard, axis, combine, identity):
    size, index = (lax.axis_size(axis), lax.axis_index(axis))
    everything = lax.all_gather(shard, axis)
    start = jnp.broadcast_to(jnp.asarray(identity, shard.dtype), shard.shape)

    def hop(k, before):
        at = size - 1 - k
        reached = at > index
        new = combine(before, everything[at])
        return jnp.where(reached, new, before)

    return lax.fori_loop(0, size, hop, start)


def permute_rows(wide, perms):
    permutations, samp_dev = perms.shape
    gene_cols = wide.shape[1]
    picked = jnp.take(wide, perms, axis=0)
    return jnp.transpose(picked, (1, 2, 0)).reshape(samp_dev, gene_cols * permutations)


def pick_rows(index, table):
    choose = (index[:, None] == jnp.arange(table.shape[0], dtype=jnp.int32)[None, :]).astype(
        jnp.float32
    )
    return jnp.dot(
        choose, table, precision=lax.Precision.HIGHEST, preferred_element_type=jnp.float32
    )


def on_device(dosage, expression, perms, windows, order):
    var_dev, samp_dev = dosage.shape
    gene_dev = expression.shape[1]
    permutations = perms.shape[0]
    samples = samp_dev * lax.axis_size("samp")
    gene_place = lax.axis_index("gene")
    samp_place = lax.axis_index("samp")
    every_sample = lax.all_gather(expression, "samp", axis=0, tiled=True)
    center = every_sample - jnp.mean(every_sample, axis=0, keepdims=True)
    scaled = center * lax.rsqrt(jnp.mean(center * center, axis=0, keepdims=True) + epsilon)
    standard = scaled.astype(jnp.bfloat16)
    wide = padded(standard, (("gene", 1),), gene_dev)
    bounds = padded(windows, (("gene", 0),), gene_dev)
    row_index = gene_place * var_dev + jnp.arange(var_dev, dtype=jnp.int32)
    gene_cols = wide.shape[1]
    columns = lax.dynamic_slice_in_dim(wide, samp_place * samp_dev, samp_dev, 0)
    shuffled = permute_rows(wide, perms)
    totals = jnp.sum(dosage.astype(jnp.float32), axis=1)
    squares = jnp.sum(jnp.square(dosage.astype(jnp.float32)), axis=1)
    direct = jnp.dot(dosage, columns, preferred_element_type=jnp.float32)
    partial_value = jnp.dot(dosage, shuffled, preferred_element_type=jnp.float32)
    partial_value, direct, totals, squares = lax.psum(
        (partial_value, direct, totals, squares), "samp"
    )
    row_mean = totals / samples
    row_var = squares / samples - row_mean * row_mean + epsilon
    row_scale = lax.rsqrt(row_var * samples)
    inside = (row_index[:, None] >= bounds[None, :, 0]) & (row_index[:, None] < bounds[None, :, 1])
    values = (
        jnp.abs(partial_value).reshape(partial_value.shape[0], gene_cols, permutations)
        * row_scale[:, None, None]
    )
    maxima = jnp.max(jnp.where(inside[:, :, None], values, jnp.float32(0.0)), axis=0)
    observed = jnp.max(
        jnp.where(inside, jnp.abs(direct) * row_scale[:, None], jnp.float32(0.0)), axis=0
    )
    width = gene_dev * permutations
    left_part = jnp.concatenate([maxima[:gene_dev].reshape(width), observed[:gene_dev]])
    right_part = jnp.concatenate([maxima[2 * gene_dev :].reshape(width), observed[2 * gene_dev :]])
    packed = jnp.stack([left_part, right_part], axis=0)
    arrived = padded(packed, (("gene", 0),), 1)
    from_left = arrived[0]
    from_right = arrived[3]
    maxima = jnp.maximum(
        maxima[gene_dev : 2 * gene_dev],
        jnp.maximum(from_left[:width], from_right[:width]).reshape(gene_dev, permutations),
    )
    observed = jnp.maximum(
        observed[gene_dev : 2 * gene_dev], jnp.maximum(from_left[width:], from_right[width:])
    )
    everyone = lax.all_gather(maxima, "gene", axis=0, tiled=True)
    my_genes = lax.dynamic_slice_in_dim(order, gene_place * gene_dev, gene_dev, 0)
    my_rows = pick_rows(my_genes, everyone)
    local_suffix = lax.cummax(my_rows, axis=0, reverse=True)
    later = prefix(local_suffix[0], "gene", jnp.maximum, jnp.zeros((permutations,), jnp.float32))
    successive = jnp.maximum(local_suffix, later[None, :])
    return (observed, successive)


def solution(mesh):
    placed = (P("gene", "samp"), P("samp", "gene"), P(None, "samp"), P("gene", None), P())
    return jax.shard_map(
        on_device,
        mesh=mesh,
        in_specs=placed,
        out_specs=(P("gene"), P("gene", None)),
        check_vma=False,
    )
```

profile of v0, /device:TPU:0, one launch (start us, length us, event | category | flops | bytes accessed | tf_op | source)
XLA Modules:
  0.0 768.2 jit_solution(72089229458095588)
XLA Ops:
  7.2 0.0 all-reduce.3.cloned.1.call-start
  7.2 15.0 %all_gather.9 = f32[5120,2]{0,1:T(2,128)S(1)} all-gather(f32[1280,2]{0,1:T(2,128)} %param.8), channel_id=1, replica_groups=mesh['gene'=8,'samp'=4] {'samp'}, dimensions={0}, use_global_device_ids=true | all-gather | bytes 51200 | tf_op jit(solution)/shard_map/all_gather | solution.py:59
  22.2 0.2 reduce_sum.36
  22.4 0.2 multiply_reduce_fusion
  22.6 0.1 multiply_convert_fusion
  22.7 0.0 copy-start.1
  22.7 1.4 collective-permute-start.3
  24.2 3.0 collective-permute-start.2
  27.2 1.2 compare_select_fusion
  28.4 0.1 broadcast_clamp_fusion
  28.5 0.0 copy-done.1
  28.5 0.2 and_bitcast_fusion
  28.7 0.0 collective-permute-done.3
  28.7 0.0 collective-permute-done.2
  28.7 0.1 pad_maximum_fusion
  28.8 0.6 copy.13
  29.4 567.2 %gather_fusion = bf16[163840,6]{1,0:T(8,128)(2,1)} fusion(bf16[5120,6]{1,0:T(8,128)(2,1)S(1)} %copy.13, s32[163840]{0:T(1024)S(1)} %broadcast_clamp_fusion), kind=kCustom, calls=%fused_computation | custom fusion | bytes 4587520 | tf_op jit(solution)/shard_map/jit(_take)/gather | solution.py:39
  596.6 31.7 %copy.14 = bf16[128,1280,6]{1,0,2:T(8,128)(2,1)} copy(bf16[128,1280,6]{2,1,0:T(8,128)(2,1)} %bitcast.39) | data formatting | bytes 3932160 | tf_op jit(solution)/shard_map/jit(_take)/gather | solution.py:39
  628.3 2.0 bitcast_select_fusion
  630.3 0.2 copy-done
  630.5 3.1 convolution_bitcast_fusion
  633.6 0.0 all-reduce.3.cloned.1.call-update
  633.6 0.7 copy-done.2
  634.3 0.1 copy.10
  634.4 1.3 collective-permute-start.1
  635.6 3.7 collective-permute-start
  639.3 0.6 fusion
  640.0 0.0 collective-permute-done.1
  640.0 0.1 collective-permute-done
  640.1 0.1 pad_add_fusion
  640.2 0.1 compare_and_fusion
  640.3 0.6 convolution_bitcast_fusion.1
  640.9 20.5 %all-reduce = (f32[768,6]{0,1:T(8,128)S(1)}, f32[768]{0:T(1024)S(1)}, f32[768]{0:T(1024)S(1)}) all-reduce(f32[768,6]{0,1:T(8,128)S(1)} %convolution_bitcast_fusion.1, f32[768]{0:T(1024)S(1)} %get-tuple-element.129, f32[768]{0:T(1024)S(1)} %get-tuple-element.128), channel_id=1, replica_groups=mesh['gene'=8,'samp'=4] {'samp'}, use_global_device_ids=true, to_apply=%region_2.3 | all-reduce | flops 6144 | bytes 49152 | tf_op jit(solution)/shard_map/psum | solution.py:73
  661.5 0.2 select_reduce_fusion.1
  661.7 0.1 fusion.11
  661.7 70.8 %all-reduce.3.cloned.1.call-done = f32[768,768]{0,1:T(8,128)} async-done(((f32[768,768]{0,1:T(8,128)}), f32[768,768]{0,1:T(8,128)}) %all-reduce.3.cloned.1.call-update) | async-done | bytes 2359312 | tf_op jit(solution)/shard_map/psum | solution.py:73
  732.6 2.1 select_reduce_fusion
  734.7 1.3 collective-permute-start.5
  736.0 3.0 collective-permute-start.4
  739.1 0.1 dynamic_slice.17
  739.1 0.0 collective-permute-done.5
  739.1 0.7 collective-permute-done.4
  739.9 12.3 %all-gather = f32[8,2,128]{2,1,0:T(2,128)S(1)} all-gather(f32[1,2,128]{2,1,0:T(2,128)S(1)} %fusion.4), channel_id=1, replica_groups=mesh['gene'=8,'samp'=4] {'gene'}, dimensions={0}, use_global_device_ids=true | all-gather | bytes 9216 | tf_op jit(solution)/shard_map/all_gather | solution.py:102
  752.1 0.2 fusion.2
  752.4 7.5 all-gather.1
  759.9 0.3 while.16
  760.2 0.6 broadcast_maximum_fusion
  760.7 0.6 fusion.7
  (28 shorter events, 0.3 us)
Async XLA Ops:
  7.2 725.4 %all-reduce.3.cloned.1.call-start = ((), (), s32[]{:S(2)}) async-start(), calls=%async_computation | async-start | bytes 4718592 | tf_op jit(solution)/shard_map/psum | solution.py:73
  22.7 5.8 copy-start.1
  22.7 6.0 collective-permute-start.3
  24.2 4.6 collective-permute-start.2
  628.3 2.1 copy-start
  633.6 0.7 copy-start.2
  634.4 5.6 collective-permute-start.1
  635.6 4.5 collective-permute-start
  640.3 98.8 %copy-start.3 = (s32[16]{0:T(128)S(1)}, s32[16]{0:T(128)}, u32[]{:S(2)}) copy-start(s32[16]{0:T(128)} %param.11) | copy-start | bytes 196
  734.7 4.5 collective-permute-start.5
  736.0 3.8 collective-permute-start.4
Sparse Core Ops, SparseCore 0:
  633.7 98.8 all-reduce.2
where the time goes:
time: 769 us; the launch traced here: 768 us
  local copies, waits for them, and re-layouts  601 us (78%)
  waiting for transfers between devices  71.7 us (9%)
  blocking collectives  55.3 us (7%)
  between operations  14.3 us (2%)
  starting transfers between devices  13.8 us (2%)
  other arithmetic  8.36 us (1%)
    gather x2, local copies, waits for them, and re-layouts, permute_rows(): picked = jnp.take(wide, perms, axis=0)  599 us
    psum x1, waiting for transfers between devices, on_device(): lax.psum((partial_value, direct, totals, squares), 'samp')  70.8 us
    psum x1, blocking collectives, on_device(): lax.psum((partial_value, direct, totals, squares), 'samp')  20.5 us
  transfers between devices with their start and end apart: 7, of which 3 were waited for; matrix products, arithmetic and copies ran while one was open for 0% of the time, Pallas kernels for 0%

commit v1 on v0

--- a/solution.py
+++ b/solution.py
@@ -102,7 +102,10 @@
     everyone = lax.all_gather(maxima, "gene", axis=0, tiled=True)
     my_genes = lax.dynamic_slice_in_dim(order, gene_place * gene_dev, gene_dev, 0)
     my_rows = pick_rows(my_genes, everyone)
-    local_suffix = lax.cummax(my_rows, axis=0, reverse=True)
+    suffix_rows = [my_rows[gene_dev - 1]]
+    for k in range(gene_dev - 2, -1, -1):
+        suffix_rows.insert(0, jnp.maximum(my_rows[k], suffix_rows[0]))
+    local_suffix = jnp.stack(suffix_rows, axis=0)
     later = prefix(local_suffix[0], "gene", jnp.maximum, jnp.zeros((permutations,), jnp.float32))
     successive = jnp.maximum(local_suffix, later[None, :])
     return (observed, successive)

time: 769 us -> 769 us (level)
  no operation moved by 1% of the time
where the time goes in v1:
time: 769 us; the launch traced here: 768 us
  local copies, waits for them, and re-layouts  601 us (78%)
  waiting for transfers between devices  71.8 us (9%)
  blocking collectives  55.4 us (7%)
  between operations  14.3 us (2%)
  starting transfers between devices  13.7 us (2%)
  other arithmetic  8.34 us (1%)
    gather x2, local copies, waits for them, and re-layouts, permute_rows(): picked = jnp.take(wide, perms, axis=0)  599 us
    psum x1, waiting for transfers between devices, on_device(): lax.psum((partial_value, direct, totals, squares), 'samp')  70.9 us
    psum x1, blocking collectives, on_device(): lax.psum((partial_value, direct, totals, squares), 'samp')  20.6 us
  transfers between devices with their start and end apart: 7, of which 3 were waited for; matrix products, arithmetic and copies ran while one was open for 0% of the time, Pallas kernels for 0%

profile of v1, /device:TPU:0, one launch (start us, length us, event | category | flops | bytes accessed | tf_op | source)
XLA Modules:
  0.0 768.2 jit_solution(16594673900540180705)
XLA Ops:
  7.2 0.0 all-reduce.3.cloned.1.call-start
  7.2 15.0 %all_gather.9 = f32[5120,2]{0,1:T(2,128)S(1)} all-gather(f32[1280,2]{0,1:T(2,128)} %param.8), channel_id=1, replica_groups=mesh['gene'=8,'samp'=4] {'samp'}, dimensions={0}, use_global_device_ids=true | all-gather | bytes 51200 | tf_op jit(solution)/shard_map/all_gather | solution.py:59
  22.2 0.2 reduce_sum.36
  22.4 0.2 multiply_reduce_fusion
  22.6 0.1 multiply_convert_fusion
  22.7 0.0 copy-start.1
  22.7 1.4 collective-permute-start.3
  24.2 3.0 collective-permute-start.2
  27.2 1.2 compare_select_fusion
  28.4 0.1 broadcast_clamp_fusion
  28.5 0.2 and_bitcast_fusion
  28.7 0.0 collective-permute-done.3
  28.7 0.0 collective-permute-done.2
  28.7 0.1 pad_maximum_fusion
  28.8 0.6 copy.13
  29.4 567.2 %gather_fusion = bf16[163840,6]{1,0:T(8,128)(2,1)} fusion(bf16[5120,6]{1,0:T(8,128)(2,1)S(1)} %copy.13, s32[163840]{0:T(1024)S(1)} %broadcast_clamp_fusion), kind=kCustom, calls=%fused_computation | custom fusion | bytes 4587520 | tf_op jit(solution)/shard_map/jit(_take)/gather | solution.py:39
  596.6 31.7 %copy.14 = bf16[128,1280,6]{1,0,2:T(8,128)(2,1)} copy(bf16[128,1280,6]{2,1,0:T(8,128)(2,1)} %bitcast.38) | data formatting | bytes 3932160 | tf_op jit(solution)/shard_map/jit(_take)/gather | solution.py:39
  628.3 2.0 bitcast_select_fusion
  630.3 0.2 copy-done
  630.5 3.1 convolution_bitcast_fusion
  633.6 0.0 all-reduce.3.cloned.1.call-update
  633.6 0.7 copy-done.2
  634.3 0.1 copy.10
  634.4 1.3 collective-permute-start.1
  635.7 3.6 collective-permute-start
  639.3 0.6 fusion
  640.0 0.0 collective-permute-done.1
  640.0 0.1 collective-permute-done
  640.1 0.1 pad_add_fusion
  640.2 0.1 compare_and_fusion
  640.3 0.6 convolution_bitcast_fusion.1
  640.9 20.6 %all-reduce = (f32[768,6]{0,1:T(8,128)S(1)}, f32[768]{0:T(1024)S(1)}, f32[768]{0:T(1024)S(1)}) all-reduce(f32[768,6]{0,1:T(8,128)S(1)} %convolution_bitcast_fusion.1, f32[768]{0:T(1024)S(1)} %get-tuple-element.129, f32[768]{0:T(1024)S(1)} %get-tuple-element.128), channel_id=1, replica_groups=mesh['gene'=8,'samp'=4] {'samp'}, use_global_device_ids=true, to_apply=%region_2.3 | all-reduce | flops 6144 | bytes 49152 | tf_op jit(solution)/shard_map/psum | solution.py:73
  661.5 0.2 select_reduce_fusion.1
  661.7 0.1 fusion.11
  661.8 70.9 %all-reduce.3.cloned.1.call-done = f32[768,768]{0,1:T(8,128)} async-done(((f32[768,768]{0,1:T(8,128)}), f32[768,768]{0,1:T(8,128)}) %all-reduce.3.cloned.1.call-update) | async-done | bytes 2359312 | tf_op jit(solution)/shard_map/psum | solution.py:73
  732.7 2.1 select_reduce_fusion
  734.8 1.3 collective-permute-start.5
  736.1 3.0 collective-permute-start.4
  739.1 0.0 copy-done.3
  739.1 0.1 dynamic_slice.17
  739.2 0.0 collective-permute-done.5
  739.2 0.7 collective-permute-done.4
  739.9 12.3 %all-gather = f32[8,2,128]{2,1,0:T(2,128)S(1)} all-gather(f32[1,2,128]{2,1,0:T(2,128)S(1)} %fusion.4), channel_id=1, replica_groups=mesh['gene'=8,'samp'=4] {'gene'}, dimensions={0}, use_global_device_ids=true | all-gather | bytes 9216 | tf_op jit(solution)/shard_map/all_gather | solution.py:102
  752.2 0.2 fusion.2
  752.4 7.5 all-gather.1
  759.9 0.3 while.16
  760.2 0.6 maximum_maximum_fusion
  760.8 0.6 fusion.7
  (27 shorter events, 0.3 us)
Async XLA Ops:
  7.2 725.5 %all-reduce.3.cloned.1.call-start = ((), (), s32[]{:S(2)}) async-start(), calls=%async_computation | async-start | bytes 4718592 | tf_op jit(solution)/shard_map/psum | solution.py:73
  22.7 5.8 copy-start.1
  22.7 6.0 collective-permute-start.3
  24.2 4.6 collective-permute-start.2
  628.3 2.1 copy-start
  633.6 0.7 copy-start.2
  634.4 5.6 collective-permute-start.1
  635.7 4.5 collective-permute-start
  640.3 98.9 %copy-start.3 = (s32[16]{0:T(128)S(1)}, s32[16]{0:T(128)}, u32[]{:S(2)}) copy-start(s32[16]{0:T(128)} %param.11) | copy-start | bytes 196
  734.8 4.5 collective-permute-start.5
  736.1 3.8 collective-permute-start.4
Sparse Core Ops, SparseCore 0:
  633.7 98.8 all-reduce.2

commit v2 on v1

--- a/solution.py
+++ b/solution.py
@@ -1,6 +1,8 @@
 import jax
 import jax.numpy as jnp
 from jax import lax
+from jax.experimental import pallas as pl
+from jax.experimental.pallas import tpu as pltpu
 from jax.sharding import PartitionSpec as P
 
 epsilon = 1e-06
@@ -33,11 +35,89 @@
     return lax.fori_loop(0, size, hop, start)
 
 
+LANES = 128
+
+
+def encode(standard):
+    value = standard.astype(jnp.float32)
+    size = jnp.abs(value)
+    down = jnp.zeros(value.shape, jnp.int32)
+    for step in (64, 32, 16, 8, 4, 2, 1):
+        small = size < 2.0 ** (7 - step)
+        size = jnp.where(small, size * 2.0**step, size)
+        down = down + jnp.where(small, step, 0)
+    mantissa = jnp.where(value < 0, -2.0 * size, 2.0 * size).astype(jnp.int32)
+    return down * 512 + mantissa + 256
+
+
+def pack_codes(wide):
+    codes = encode(wide).T
+    words = codes[0::2] + (codes[1::2] << 16)
+    return words.reshape(words.shape[0], -1, LANES)
+
+
+def powers():
+    lane = lax.broadcasted_iota(jnp.int32, (16, LANES), 1)
+    power = jnp.full((16, LANES), 0.5, jnp.float32)
+    for step in (64, 32, 16, 8, 4, 2, 1):
+        power = jnp.where((lane & step) != 0, power * 2.0**-step, power)
+    return jnp.where(lane >= 126, 0.0, power)
+
+
+def pick(table, index):
+    return jnp.take_along_axis(table, index, axis=1)
+
+
+def shuffle_tile(table_ref, index, words, rows):
+    low = index & (LANES - 1)
+    high = index >> 7
+    shape = index.shape
+    found = [jnp.zeros(shape, jnp.int32) for _ in range(words)]
+    for row in range(rows):
+        here = high == row
+        for word in range(words):
+            entry = jnp.broadcast_to(table_ref[word, pl.ds(row, 1), :], shape)
+            found[word] = jnp.where(here, pick(entry, low), found[word])
+    return found
+
+
+def decode(code, power):
+    mantissa = ((code & 511) - 256).astype(jnp.float32)
+    return (mantissa * pick(power, (code >> 9) & 127)).astype(jnp.bfloat16)
+
+
+def shuffle_kernel(table_ref, perms_ref, out_ref):
+    words, rows, _ = table_ref.shape
+    permutations, samp_dev = perms_ref.shape
+    power = powers()
+    across = samp_dev // LANES
+
+    def tile(t, carry):
+        p = pl.multiple_of((t // across) * 16, 16)
+        s = pl.multiple_of((t % across) * LANES, LANES)
+        index = perms_ref[pl.ds(p, 16), pl.ds(s, LANES)]
+        found = shuffle_tile(table_ref, index, words, rows)
+        for word in range(words):
+            out_ref[2 * word, pl.ds(p, 16), pl.ds(s, LANES)] = decode(found[word], power)
+            out_ref[2 * word + 1, pl.ds(p, 16), pl.ds(s, LANES)] = decode(
+                found[word] >> 16, power
+            )
+        return carry
+
+    lax.fori_loop(0, permutations // 16 * across, tile, 0)
+
+
 def permute_rows(wide, perms):
     permutations, samp_dev = perms.shape
-    gene_cols = wide.shape[1]
-    picked = jnp.take(wide, perms, axis=0)
-    return jnp.transpose(picked, (1, 2, 0)).reshape(samp_dev, gene_cols * permutations)
+    genes = wide.shape[1]
+    out = pl.pallas_call(
+        shuffle_kernel,
+        out_shape=jax.ShapeDtypeStruct((genes, permutations, samp_dev), jnp.bfloat16),
+        in_specs=[pl.BlockSpec(memory_space=pltpu.VMEM)] * 2,
+        out_specs=pl.BlockSpec(memory_space=pltpu.VMEM),
+        compiler_params=pltpu.CompilerParams(vmem_limit_bytes=32 * 2**20),
+    )(pack_codes(wide), perms)
+    return out.reshape(genes * permutations, samp_dev)
 
 
 def pick_rows(index, table):
@@ -69,7 +149,9 @@
     totals = jnp.sum(dosage.astype(jnp.float32), axis=1)
     squares = jnp.sum(jnp.square(dosage.astype(jnp.float32)), axis=1)
     direct = jnp.dot(dosage, columns, preferred_element_type=jnp.float32)
-    partial_value = jnp.dot(dosage, shuffled, preferred_element_type=jnp.float32)
+    partial_value = lax.dot_general(
+        dosage, shuffled, (((1,), (1,)), ((), ())), preferred_element_type=jnp.float32
+    )
     partial_value, direct, totals, squares = lax.psum(
         (partial_value, direct, totals, squares), "samp"
     )

time: 769 us -> 204 us (0.27)
  local copies, waits for them, and re-layouts: 601 us -> 2.25 us
  Pallas kernels: 0 us -> 35.1 us
    gather x2 -> x0, local copies, waits for them, and re-layouts: 599 us -> none  [permute_rows(): picked = jnp.take(wide, perms, axis=0)]
    pallas_call x0 -> x1, Pallas kernels: none -> 35.1 us  [permute_rows(): pl.pallas_call(shuffle_kernel, out_shape=jax.ShapeDtypeStruct((genes, per...]
  transfers between devices with their start and end apart: 7 -> 7, of which waited for: 3 -> 4; matrix products, arithmetic and copies ran while one was open for 0% -> 1% of each run, Pallas kernels for 0% -> 0%
where the time goes in v2:
time: 204 us; the launch traced here: 203 us
  waiting for transfers between devices  73.2 us (36%)
  blocking collectives  55.3 us (27%)
  Pallas kernels  35.1 us (17%)
  between operations  14.3 us (7%)
  starting transfers between devices  13.7 us (7%)
  other arithmetic  5.26 us (3%)
  matrix products  3.93 us (2%)
  local copies, waits for them, and re-layouts  2.25 us (1%)
    psum x1, waiting for transfers between devices, on_device(): lax.psum((partial_value, direct, totals, squares), 'samp')  71.5 us
    pallas_call x1, Pallas kernels, permute_rows(): pl.pallas_call(shuffle_kernel, out_shape=jax.ShapeDtypeStruct((genes, per...  35.1 us
    psum x1, blocking collectives, on_device(): lax.psum((partial_value, direct, totals, squares), 'samp')  20.5 us
    all_gather x1, blocking collectives, on_device(): every_sample = lax.all_gather(expression, 'samp', axis=0, tiled=True)  15 us
    all_gather x1, blocking collectives, on_device(): everyone = lax.all_gather(maxima, 'gene', axis=0, tiled=True)  12.3 us
    ppermute x3, starting transfers between devices, padded(): lax.ppermute(lax.slice_in_dim(block, block.shape[dim] - width, None, axis...  9.77 us
    all_gather x1, blocking collectives, prefix(): everything = lax.all_gather(shard, axis)  7.52 us
  transfers between devices with their start and end apart: 7, of which 4 were waited for; matrix products, arithmetic and copies ran while one was open for 1% of the time, Pallas kernels for 0%

profile of v2, /device:TPU:0, one launch (start us, length us, event | category | flops | bytes accessed | tf_op | source)
XLA Modules:
  0.0 203.1 jit_solution(2324719959698895105)
XLA Ops:
  7.2 0.0 all-reduce.3.cloned.1.call-start
  7.2 15.0 %all_gather.9 = f32[5120,2]{0,1:T(2,128)S(1)} all-gather(f32[1280,2]{0,1:T(2,128)} %param.8), channel_id=1, replica_groups=mesh['gene'=8,'samp'=4] {'samp'}, dimensions={0}, use_global_device_ids=true | all-gather | bytes 51200 | tf_op jit(solution)/shard_map/all_gather | solution.py:139
  22.2 0.2 reduce_sum.36
  22.4 0.2 multiply_reduce_fusion
  22.6 0.1 multiply_convert_fusion
  22.7 1.3 collective-permute-start.3
  24.0 3.0 %collective-permute-start.2 = (bf16[5120,2]{0,1:T(2,128)(2,1)S(1)}, bf16[5120,2]{0,1:T(2,128)(2,1)S(1)}, u32[]{:S(2)}, u32[]{:S(2)}) collective-permute-start(bf16[5120,2]{0,1:T(2,128)(2,1)S(1)} %multiply_convert_fusion), channel_id=1, source_target_pairs={{0,4},{4,8},{8,12},{12,16},{16,20},{20,24},{24,28},{1,5},{5,9},{9,... | collective-permute-start | bytes 61448 | tf_op jit(solution)/shard_map/ppermute | solution.py:16
  27.1 0.0 collective-permute-done.3
  27.1 0.8 collective-permute-done.2
  27.9 0.3 fusion.10
  28.2 0.1 slice.66
  28.3 0.1 slice.67
  28.5 0.0 copy-start
  28.5 1.1 copy-done
  29.6 0.0 copy-start.1
  29.6 35.1 %shard_map.68 = bf16[6,128,1280]{2,1,0:T(8,128)(2,1)S(1)} custom-call(s32[3,40,128]{2,1,0:T(8,128)S(1)} %bitcast.41, s32[128,1280]{1,0:T(8,128)S(1)} %copy-done), custom_call_target="tpu_custom_call" | custom-call | tf_op jit(solution)/shard_map/pallas_call | solution.py:113
  64.7 0.0 copy-done.1
  64.7 3.1 %convolution_bitcast_fusion = f32[768,768]{0,1:T(8,128)} fusion(bf16[768,1280]{1,0:T(8,128)(2,1)S(1)} %bitcast.40, bf16[768,1280]{1,0:T(8,128)(2,1)S(1)} %copy-done.1), kind=kOutput, calls=%fused_computation.6 | convolution fusion | flops 1509949440 | bytes 6291456 | tf_op jit(solution)/shard_map/dot_general | solution.py:152
  67.8 0.0 all-reduce.3.cloned.1.call-update
  67.9 0.7 copy-done.2
  68.5 0.1 copy.7
  68.6 1.3 collective-permute-start.1
  69.9 3.7 %collective-permute-start = (s32[2,2]{0,1:T(2,128)S(1)}, s32[2,2]{0,1:T(2,128)S(1)}, u32[]{:S(2)}, u32[]{:S(2)}) collective-permute-start(s32[2,2]{0,1:T(2,128)S(1)} %copy.7), channel_id=1, source_target_pairs={{0,4},{4,8},{8,12},{12,16},{16,20},{20,24},{24,28},{1,5},{5,9},{9,... | collective-permute-start | bytes 56 | tf_op jit(solution)/shard_map/ppermute | solution.py:16
  73.6 0.6 fusion
  74.3 0.0 collective-permute-done.1
  74.3 0.1 collective-permute-done
  74.4 0.1 pad_add_fusion
  74.5 0.1 compare_and_fusion
  74.6 0.1 pad_maximum_fusion
  74.7 0.0 copy-start.3
  74.7 0.6 convolution_bitcast_fusion.1
  75.3 20.5 %all-reduce = (f32[768,6]{0,1:T(8,128)S(1)}, f32[768]{0:T(1024)S(1)}, f32[768]{0:T(1024)S(1)}) all-reduce(f32[768,6]{0,1:T(8,128)S(1)} %convolution_bitcast_fusion.1, f32[768]{0:T(1024)S(1)} %get-tuple-element.129, f32[768]{0:T(1024)S(1)} %get-tuple-element.128), channel_id=1, replica_groups=mesh['gene'=8,'samp'=4] {'samp'}, use_global_device_ids=true, to_apply=%region_2.3 | all-reduce | flops 6144 | bytes 49152 | tf_op jit(solution)/shard_map/psum | solution.py:155
  95.8 0.2 select_reduce_fusion.1
  96.0 0.1 fusion.21
  96.0 71.5 %all-reduce.3.cloned.1.call-done = f32[768,768]{0,1:T(8,128)} async-done(((f32[768,768]{0,1:T(8,128)}), f32[768,768]{0,1:T(8,128)}) %all-reduce.3.cloned.1.call-update) | async-done | bytes 2359312 | tf_op jit(solution)/shard_map/psum | solution.py:155
  167.5 2.1 %select_reduce_fusion = f32[768]{0:T(1024)S(1)} fusion(f32[768,768]{0,1:T(8,128)} %all-reduce.3.cloned.1.call-done, f32[768]{0:T(1024)S(1)} %multiply_rsqrt_fusion, pred[768,6]{0,1:T(8,128)(4,1)S(1)} %compare_and_fusion), kind=kLoop, calls=%fused_computation.5 | loop fusion | flops 2358528 | bytes 2370048 | tf_op jit(solution)/shard_map/reduce_max | solution.py:166
  169.6 1.3 collective-permute-start.5
  171.0 3.0 %collective-permute-start.4 = (f32[1,258]{1,0:T(1,128)S(1)}, f32[1,258]{1,0:T(1,128)S(1)}, u32[]{:S(2)}, u32[]{:S(2)}) collective-permute-start(f32[1,258]{1,0:T(1,128)S(1)} %stack.10), channel_id=1, source_target_pairs={{0,4},{4,8},{8,12},{12,16},{16,20},{20,24},{24,28},{1,5},{5,9},{9,... | collective-permute-start | bytes 3104 | tf_op jit(solution)/shard_map/ppermute | solution.py:16
  174.0 0.0 copy-done.3
  174.0 0.1 dynamic_slice.17
  174.1 0.0 collective-permute-done.5
  174.1 0.7 collective-permute-done.4
  174.8 12.3 %all-gather = f32[8,2,128]{2,1,0:T(2,128)S(1)} all-gather(f32[1,2,128]{2,1,0:T(2,128)S(1)} %fusion.14), channel_id=1, replica_groups=mesh['gene'=8,'samp'=4] {'gene'}, dimensions={0}, use_global_device_ids=true | all-gather | bytes 9216 | tf_op jit(solution)/shard_map/all_gather | solution.py:184
  187.1 0.2 fusion.12
  187.3 7.5 %all-gather.1 = f32[8,1,128]{2,1,0:T(1,128)S(1)} all-gather(f32[1,1,128]{2,1,0:T(1,128)S(1)} %bitcast.44), channel_id=1, replica_groups=mesh['gene'=8,'samp'=4] {'gene'}, dimensions={0}, use_global_device_ids=true | all-gather | bytes 4608 | tf_op jit(solution)/shard_map/all_gather | solution.py:26
  194.8 0.3 while.16
  195.1 0.6 maximum_maximum_fusion
  195.7 0.6 fusion.17
  (25 shorter events, 0.3 us)
Async XLA Ops:
  7.2 160.4 %all-reduce.3.cloned.1.call-start = ((), (), s32[]{:S(2)}) async-start(), calls=%async_computation | async-start | bytes 4718592 | tf_op jit(solution)/shard_map/psum | solution.py:155
  22.7 4.3 %collective-permute-start.3 = (bf16[5120,2]{0,1:T(2,128)(2,1)S(1)}, bf16[5120,2]{0,1:T(2,128)(2,1)S(1)}, u32[]{:S(2)}, u32[]{:S(2)}) collective-permute-start(bf16[5120,2]{0,1:T(2,128)(2,1)S(1)} %multiply_convert_fusion), channel_id=1, source_target_pairs={{4,0},{8,4},{12,8},{16,12},{20,16},{24,20},{28,24},{5,1},{9,5},{13... | collective-permute-start | bytes 61448 | tf_op jit(solution)/shard_map/ppermute | solution.py:19
  24.0 3.9 %collective-permute-start.2 = (bf16[5120,2]{0,1:T(2,128)(2,1)S(1)}, bf16[5120,2]{0,1:T(2,128)(2,1)S(1)}, u32[]{:S(2)}, u32[]{:S(2)}) collective-permute-start(bf16[5120,2]{0,1:T(2,128)(2,1)S(1)} %multiply_convert_fusion), channel_id=1, source_target_pairs={{0,4},{4,8},{8,12},{12,16},{16,20},{20,24},{24,28},{1,5},{5,9},{9,... | collective-permute-start | bytes 61448 | tf_op jit(solution)/shard_map/ppermute | solution.py:16
  28.5 1.1 copy-start
  29.6 35.1 %copy-start.1 = (bf16[768,1280]{1,0:T(8,128)(2,1)S(1)}, bf16[768,1280]{1,0:T(8,128)(2,1)}, u32[]{:S(2)}) copy-start(bf16[768,1280]{1,0:T(8,128)(2,1)} %param.7) | copy-start | bytes 5898244
  67.8 0.7 copy-start.2
  68.6 5.7 %collective-permute-start.1 = (s32[2,2]{0,1:T(2,128)S(1)}, s32[2,2]{0,1:T(2,128)S(1)}, u32[]{:S(2)}, u32[]{:S(2)}) collective-permute-start(s32[2,2]{0,1:T(2,128)S(1)} %copy.7), channel_id=1, source_target_pairs={{4,0},{8,4},{12,8},{16,12},{20,16},{24,20},{28,24},{5,1},{9,5},{13... | collective-permute-start | bytes 56 | tf_op jit(solution)/shard_map/ppermute | solution.py:19
  69.9 4.5 %collective-permute-start = (s32[2,2]{0,1:T(2,128)S(1)}, s32[2,2]{0,1:T(2,128)S(1)}, u32[]{:S(2)}, u32[]{:S(2)}) collective-permute-start(s32[2,2]{0,1:T(2,128)S(1)} %copy.7), channel_id=1, source_target_pairs={{0,4},{4,8},{8,12},{12,16},{16,20},{20,24},{24,28},{1,5},{5,9},{9,... | collective-permute-start | bytes 56 | tf_op jit(solution)/shard_map/ppermute | solution.py:16
  74.7 99.4 %copy-start.3 = (s32[16]{0:T(128)S(1)}, s32[16]{0:T(128)}, u32[]{:S(2)}) copy-start(s32[16]{0:T(128)} %param.11) | copy-start | bytes 196
  169.6 4.5 %collective-permute-start.5 = (f32[1,258]{1,0:T(1,128)S(1)}, f32[1,258]{1,0:T(1,128)S(1)}, u32[]{:S(2)}, u32[]{:S(2)}) collective-permute-start(f32[1,258]{1,0:T(1,128)S(1)} %stack.11), channel_id=1, source_target_pairs={{4,0},{8,4},{12,8},{16,12},{20,16},{24,20},{28,24},{5,1},{9,5},{13... | collective-permute-start | bytes 3104 | tf_op jit(solution)/shard_map/ppermute | solution.py:19
  171.0 3.8 %collective-permute-start.4 = (f32[1,258]{1,0:T(1,128)S(1)}, f32[1,258]{1,0:T(1,128)S(1)}, u32[]{:S(2)}, u32[]{:S(2)}) collective-permute-start(f32[1,258]{1,0:T(1,128)S(1)} %stack.10), channel_id=1, source_target_pairs={{0,4},{4,8},{8,12},{12,16},{16,20},{20,24},{24,28},{1,5},{5,9},{9,... | collective-permute-start | bytes 3104 | tf_op jit(solution)/shard_map/ppermute | solution.py:16
Sparse Core Ops, SparseCore 0:
  68.0 99.5 all-reduce.2

commit v3 on v0

v3 whole, which is shorter than its diff:
```python
import functools

import jax
import jax.numpy as jnp
from jax import lax
from jax.experimental import pallas as pl
from jax.experimental.pallas import tpu as pltpu
from jax.sharding import PartitionSpec as P

epsilon = 1e-06


LANES = 128


def encode(value):
    size = jnp.abs(value)
    down = jnp.zeros(value.shape, jnp.int32)
    for step in (64, 32, 16, 8, 4, 2, 1):
        small = size < 2.0 ** (7 - step)
        size = jnp.where(small, size * 2.0**step, size)
        down = down + jnp.where(small, step, 0)
    mantissa = jnp.where(value < 0, -2.0 * size, 2.0 * size).astype(jnp.int32)
    return down * 512 + mantissa + 256


def powers():
    lane = lax.broadcasted_iota(jnp.int32, (16, LANES), 1)
    power = jnp.full((16, LANES), 0.5, jnp.float32)
    for step in (64, 32, 16, 8, 4, 2, 1):
        power = jnp.where((lane & step) != 0, power * 2.0**-step, power)
    return jnp.where(lane >= 126, 0.0, power)


def pick(table, index):
    return jnp.take_along_axis(table, index, axis=1)


def decode(code, power):
    mantissa = ((code & 511) - 256).astype(jnp.float32)
    return (mantissa * pick(power, (code >> 9) & 127)).astype(jnp.bfloat16)


def rows_dot(left, right):
    return lax.dot_general(left, right, (((1,), (1,)), ((), ())), preferred_element_type=jnp.float32)


def whole_sum(block):
    return jnp.sum(jnp.sum(block, axis=0, keepdims=True), axis=1, keepdims=True)


def scan_kernel(
    gene_size,
    samp_size,
    samples,
    message_ref,
    dosage_ref,
    perms_ref,
    out_ref,
    arrived,
    table,
    alone,
    moments,
    directs,
    shuffled,
    mine,
    outgoing,
    incoming,
    peaks,
    rows_z,
    message_send,
    message_recv,
    moment_send,
    moment_recv,
    direct_send,
    direct_recv,
    block_send,
    block_recv,
    row_send,
    row_recv,
    all_send,
    all_recv,
):
    var_dev, samp_dev = dosage_ref.shape
    permutations = perms_ref.shape[0]
    gene_dev = message_ref.shape[0]
    genes = 3 * gene_dev
    share = permutations // samp_size
    across = samp_dev // LANES
    g = lax.axis_index("gene")
    z = lax.axis_index("samp")

    def there(dg, dz):
        return {
            "gene": lax.rem(g + dg + gene_size, gene_size),
            "samp": lax.rem(z + dz, samp_size),
        }

    def send(source, target, send_sem, recv_sem, device):
        return pltpu.make_async_remote_copy(
            src_ref=source,
            dst_ref=target,
            send_sem=send_sem,
            recv_sem=recv_sem,
            device_id=device,
            device_id_type=pl.DeviceIdType.MESH,
        )

    near = [(dg, dz) for dz in range(samp_size) for dg in (-1, 0, 1) if (dg, dz) != (0, 0)]
    far = [(dg, 0) for dg in range(2, gene_size - 1)]
    barrier = pltpu.get_barrier_semaphore()
    for dg, dz in near + far:
        pl.semaphore_signal(
            barrier, inc=1, device_id=there(dg, dz), device_id_type=pl.DeviceIdType.MESH
        )
    pl.semaphore_wait(barrier, len(near + far))

    pending = []
    for dg, dz in near:
        copy = send(
            message_ref,
            arrived.at[1 - dg, z],
            message_send.at[1 - dg, dz],
            message_recv.at[1 - dg, z],
            there(dg, dz),
        )
        copy.start()
        pending.append(copy)
    arrived[1, z] = message_ref[...]

    ones = jnp.ones((16, samp_dev), jnp.bfloat16)
    step = 256 if var_dev % 256 == 0 else var_dev
    for v in range(0, var_dev, step):
        part = dosage_ref[v : v + step, :]
        wide = part.astype(jnp.float32)
        square = wide * wide
        upper = square.astype(jnp.bfloat16)
        lower = (square - upper.astype(jnp.float32)).astype(jnp.bfloat16)
        moments[z, 0:8, v : v + step] = rows_dot(ones, part)[0:8]
        moments[z, 8:16, v : v + step] = (rows_dot(ones, upper) + rows_dot(ones, lower))[0:8]
    for dz in range(1, samp_size):
        copy = send(
            moments.at[z], moments.at[z], moment_send.at[dz], moment_recv.at[z], there(0, dz)
        )
        copy.start()
        pending.append(copy)

    for r in (0, 1, 2):
        for dz in range(samp_size):
            if (r, dz) != (1, 0):
                source = lax.rem(z + dz, samp_size)
                send(
                    message_ref,
                    arrived.at[r, source],
                    message_send.at[r, dz],
                    message_recv.at[r, source],
                    there(0, 1),
                ).wait_recv()

    alone[...] = jnp.zeros_like(alone)
    sums = []
    for r in range(3):
        for pair in range(gene_dev // 2):
            codes = [[], []]
            for half in range(2):
                j = 2 * pair + half
                blocks = [arrived[r, k, j, 0:across, :] for k in range(samp_size)]
                mean = whole_sum(sum(blocks)) / samples
                spread = whole_sum(sum(jnp.square(k - mean) for k in blocks)) / samples
                factor = lax.rsqrt(spread + epsilon)
                total = jnp.zeros((across, LANES), jnp.float32)
                for k in range(samp_size):
                    value = ((blocks[k] - mean) * factor).astype(jnp.bfloat16).astype(jnp.float32)
                    total = total + value
                    codes[half].append(encode(value))
                sums.append(whole_sum(total))
                own = (arrived[r, z, j, 0:across, :] - mean) * factor
                own = own.astype(jnp.bfloat16).astype(jnp.float32)
                row = r * gene_dev + j
                for h in range(across):
                    alone[row : row + 1, h * LANES : (h + 1) * LANES] = own[h : h + 1, :]
            word = r * (gene_dev // 2) + pair
            for k in range(samp_size):
                table[word, k, 0:across, :] = codes[0][k] + (codes[1][k] << 16)

    each = alone[...].astype(jnp.bfloat16)
    for v in range(0, var_dev, step):
        directs[z, :, v : v + step] = rows_dot(each, dosage_ref[v : v + step, :])
    for dz in range(1, samp_size):
        copy = send(
            directs.at[z], directs.at[z], direct_send.at[dz], direct_recv.at[z], there(0, dz)
        )
        copy.start()
        pending.append(copy)

    for dz in range(1, samp_size):
        source = lax.rem(z + dz, samp_size)
        send(
            moments.at[z],
            moments.at[source],
            moment_send.at[dz],
            moment_recv.at[source],
            there(0, dz),
        ).wait_recv()
    totals = sum(moments[k, 0:1, :] for k in range(samp_size))
    squares = sum(moments[k, 8:9, :] for k in range(samp_size))
    row_mean = totals / samples
    row_scale = lax.rsqrt((squares / samples - row_mean * row_mean + epsilon) * samples)

    power = powers()
    words = table.shape[0]

    def block(target):
        first = pl.multiple_of(target * share, share)

        def tile(t, carry):
            p = pl.multiple_of((t // across) * 16, 16)
            s = pl.multiple_of((t % across) * LANES, LANES)
            index = perms_ref[pl.ds(pl.multiple_of(first + p, 16), 16), pl.ds(s, LANES)]
            low = index & (LANES - 1)
            high = index >> 7
            found = [jnp.zeros(index.shape, jnp.int32) for _ in range(words)]
            for k in range(samp_size):
                for h in range(across):
                    here = high == k * across + h
                    for w in range(words):
                        entry = jnp.broadcast_to(table[w, k, h : h + 1, :], index.shape)
                        found[w] = jnp.where(here, pick(entry, low), found[w])
            for w in range(words):
                for half in range(2):
                    row = pl.multiple_of((2 * w + half) * share + p, 16)
                    shuffled[pl.ds(row, 16), pl.ds(s, LANES)] = decode(
                        found[w] >> (16 * half), power
                    )
            return carry

        lax.fori_loop(0, share // 16 * across, tile, 0)
        taken = shuffled[...]
        column = jnp.sum(taken.astype(jnp.float32), axis=1, keepdims=True)
        for v in range(0, var_dev, step):
            mine[:, v : v + step] = (
                rows_dot(taken, dosage_ref[v : v + step, :]) - column * row_mean[:, v : v + step]
            )

    def remote(k, carry):
        target = lax.rem(z + 1 + k, samp_size)
        block(target)
        outgoing[k] = mine[...].astype(jnp.bfloat16)
        send(
            outgoing.at[k],
            incoming.at[k],
            block_send.at[k],
            block_recv.at[k],
            {"gene": g, "samp": target},
        ).start()
        return carry

    lax.fori_loop(0, samp_size - 1, remote, 0)
    block(z)

    for dz in range(1, samp_size):
        source = lax.rem(z + dz, samp_size)
        send(
            directs.at[z],
            directs.at[source],
            direct_send.at[dz],
            direct_recv.at[source],
            there(0, dz),
        ).wait_recv()
    direct = sum(directs[k] for k in range(samp_size))
    place = (g * var_dev + lax.broadcasted_iota(jnp.int32, (1, var_dev), 1)).astype(jnp.float32)
    peaks[...] = jnp.zeros_like(peaks)
    for k in range(samp_size - 1):
        send(
            outgoing.at[k], incoming.at[k], block_send.at[k], block_recv.at[k], there(0, k + 1)
        ).wait()

    def fold(values):
        best = values[:, 0:LANES]
        for t in range(LANES, var_dev, LANES):
            best = jnp.maximum(best, values[:, t : t + LANES])
        return best

    for row in range(genes):
        r, j = row // gene_dev, row % gene_dev
        start = arrived[r, 0, j, across : across + 1, 0:1]
        finish = arrived[r, 0, j, across + 1 : across + 2, 0:1]
        weight = jnp.where((place >= start) & (place < finish), row_scale, 0.0)
        rows = slice(row * share, (row + 1) * share)
        total = mine[rows, :] + row_mean * sums[row]
        for k in range(samp_size - 1):
            total = total + incoming[k, rows, :].astype(jnp.float32)
        peaks[rows, :] = fold(jnp.abs(total) * weight)
        last = genes * share + row
        peaks[last : last + 1, :] = fold(jnp.abs(direct[row : row + 1, :]) * weight)
    rows_z[z] = jnp.max(peaks[...].T, axis=0, keepdims=True)
    for dz in range(1, samp_size):
        copy = send(rows_z.at[z], rows_z.at[z], row_send.at[dz], row_recv.at[z], there(0, dz))
        copy.start()
        pending.append(copy)
    for dz in range(1, samp_size):
        source = lax.rem(z + dz, samp_size)
        send(
            rows_z.at[z], rows_z.at[source], row_send.at[dz], row_recv.at[source], there(0, dz)
        ).wait_recv()
    for dg in range(1, gene_size):
        copy = send(rows_z, out_ref.at[g], all_send.at[dg], all_recv.at[g], there(dg, 0))
        copy.start()
        pending.append(copy)
    out_ref[g] = rows_z[...]
    for dg in range(1, gene_size):
        source = lax.rem(g + dg, gene_size)
        send(
            rows_z, out_ref.at[source], all_send.at[dg], all_recv.at[source], there(dg, 0)
        ).wait_recv()
    for copy in pending:
        copy.wait_send()


def up_to(size, unit):
    return -(-size // unit) * unit


def scan(dosage, expression, perms, windows):
    var_dev, samp_dev = dosage.shape
    gene_dev = expression.shape[1]
    permutations = perms.shape[0]
    gene_size, samp_size = lax.axis_size("gene"), lax.axis_size("samp")
    genes = 3 * gene_dev
    across = samp_dev // LANES
    share = permutations // samp_size
    height = up_to(across + 2, 8)
    lines = jnp.concatenate(
        [
            expression.T.reshape(gene_dev, across, LANES),
            jnp.broadcast_to(
                windows.astype(jnp.float32)[:, :, None], (gene_dev, 2, LANES)
            ),
            jnp.zeros((gene_dev, height - across - 2, LANES), jnp.float32),
        ],
        axis=1,
    )
    width = up_to(genes * share + genes, LANES)
    few = up_to(genes, 16)
    dma = pltpu.SemaphoreType.DMA
    kernel = functools.partial(scan_kernel, gene_size, samp_size, samp_dev * samp_size)
    return pl.pallas_call(
        kernel,
        out_shape=jax.ShapeDtypeStruct((gene_size, samp_size, 1, width), jnp.float32),
        in_specs=[pl.BlockSpec(memory_space=pltpu.VMEM)] * 3,
        out_specs=pl.BlockSpec(memory_space=pltpu.VMEM),
        scratch_shapes=[
            pltpu.VMEM((3, samp_size, gene_dev, height, LANES), jnp.float32),
            pltpu.VMEM((genes // 2, samp_size, up_to(across, 8), LANES), jnp.int32),
            pltpu.VMEM((few, samp_dev), jnp.float32),
            pltpu.VMEM((samp_size, 16, var_dev), jnp.float32),
            pltpu.VMEM((samp_size, few, var_dev), jnp.float32),
            pltpu.VMEM((genes * share, samp_dev), jnp.bfloat16),
            pltpu.VMEM((genes * share, var_dev), jnp.float32),
            pltpu.VMEM((samp_size - 1, genes * share, var_dev), jnp.bfloat16),
            pltpu.VMEM((samp_size - 1, genes * share, var_dev), jnp.bfloat16),
            pltpu.VMEM((width, LANES), jnp.float32),
            pltpu.VMEM((samp_size, 1, width), jnp.float32),
            dma((3, samp_size)),
            dma((3, samp_size)),
        ]
        + [dma((samp_size,))] * 8
        + [dma((gene_size,))] * 2,
        compiler_params=pltpu.CompilerParams(
            collective_id=0, has_side_effects=True, vmem_limit_bytes=48 * 2**20
        ),
    )(lines, dosage, perms)


def on_device(dosage, expression, perms, windows, order):
    gene_dev = expression.shape[1]
    permutations = perms.shape[0]
    gene_size, samp_size = lax.axis_size("gene"), lax.axis_size("samp")
    gene_place = lax.axis_index("gene")
    share = permutations // samp_size
    genes = 3 * gene_dev
    found = scan(dosage, expression, perms, windows)[:, :, 0, :]
    maxima = found[:, :, : genes * share].reshape(gene_size, samp_size, 3, gene_dev, share)
    maxima = maxima.transpose(0, 2, 3, 1, 4).reshape(gene_size, 3, gene_dev, permutations)
    seen = found[:, 0, genes * share : genes * share + genes].reshape(gene_size, 3, gene_dev, 1)
    every = jnp.concatenate([maxima, seen], axis=3)
    every = jnp.maximum(
        every[:, 1],
        jnp.maximum(jnp.roll(every[:, 0], -1, axis=0), jnp.roll(every[:, 2], 1, axis=0)),
    )
    observed = lax.dynamic_slice_in_dim(every[:, :, permutations], gene_place, 1, 0)[0]
    ranked = every[:, :, :permutations].reshape(gene_size * gene_dev, permutations)
    ids = jnp.arange(order.shape[0], dtype=jnp.int32)
    rank = jnp.sum(jnp.where(order[None, :] == ids[:, None], ids[None, :], 0), axis=1)
    mine = gene_place * gene_dev + jnp.arange(gene_dev, dtype=jnp.int32)
    later = rank[None, :] >= mine[:, None]
    successive = jnp.max(jnp.where(later[:, :, None], ranked[None], 0.0), axis=1)
    return (observed, successive)


def solution(mesh):
    placed = (P("gene", "samp"), P("samp", "gene"), P(None, "samp"), P("gene", None), P())
    return jax.shard_map(
        on_device,
        mesh=mesh,
        in_specs=placed,
        out_specs=(P("gene"), P("gene", None)),
        check_vma=False,
    )
```

time: 769 us -> 70.9 us (0.09)
  local copies, waits for them, and re-layouts: 601 us -> 4.7 us
  waiting for transfers between devices: 71.7 us -> 0 us
  Pallas kernels: 0 us -> 63.6 us
  blocking collectives: 55.3 us -> 0 us
  starting transfers between devices: 13.8 us -> 0 us
  between operations: 14.3 us -> 0.73 us
    gather x2 -> x0, local copies, waits for them, and re-layouts: 599 us -> none  [permute_rows(): picked = jnp.take(wide, perms, axis=0)]
    psum x1 -> x0, waiting for transfers between devices: 70.8 us -> none  [on_device(): lax.psum((partial_value, direct, totals, squares), 'samp')]
    pallas_call x0 -> x1, Pallas kernels: none -> 63.6 us  [scan(): pl.pallas_call(kernel, out_shape=jax.ShapeDtypeStruct((gene_size, samp_si...]
    all_gather x3 -> x0, blocking collectives: 34.8 us -> none  [the longest x1 15 us: on_device(): every_sample = lax.all_gather(expression, 'samp', axis=0, tiled=True)]
    psum x1 -> x0, blocking collectives: 20.5 us -> none  [on_device(): lax.psum((partial_value, direct, totals, squares), 'samp')]
    ppermute x6 -> x0, starting transfers between devices: 13.7 us -> none  [the longest x3 9.72 us: padded(): lax.ppermute(lax.slice_in_dim(block, block.shape[dim] - width, None, axis...]
  transfers between devices with their start and end apart: 7 -> 0, of which waited for: 3 -> 0; matrix products, arithmetic and copies ran while one was open for 0% -> 0% of each run, Pallas kernels for 0% -> 0%
where the time goes in v3:
time: 70.9 us; the launch traced here: 70.7 us
  Pallas kernels  63.6 us (90%)
  local copies, waits for them, and re-layouts  4.7 us (7%)
  other arithmetic  1.66 us (2%)
  between operations  0.73 us (1%)
    pallas_call x1, Pallas kernels, scan(): pl.pallas_call(kernel, out_shape=jax.ShapeDtypeStruct((gene_size, samp_si...  63.6 us
    unnamed x7, local copies, waits for them, and re-layouts  2.65 us

profile of v3, /device:TPU:0, one launch (start us, length us, event | category | flops | bytes accessed | tf_op | source)
XLA Modules:
  0.0 70.7 jit_solution(12673485793851713463)
XLA Ops:
  0.6 0.0 copy-start.2
  0.6 0.7 convert_element_type.3
  1.3 0.1 broadcast_in_dim.49
  1.4 0.7 %reshape.52 = f32[2,10,128]{2,1,0:T(8,128)S(1)} reshape(f32[2,1280]{1,0:T(2,128)} %bitcast.25) | data formatting | bytes 20480 | tf_op jit(solution)/shard_map/reshape | solution.py:335
  2.1 0.1 pad.8.clone
  2.2 0.1 maximum_maximum_fusion.message_ref
  2.3 0.0 copy-start
  2.3 1.5 %copy-done = bf16[768,1280]{1,0:T(8,128)(2,1)S(1)} copy-done((bf16[768,1280]{1,0:T(8,128)(2,1)S(1)}, bf16[768,1280]{1,0:T(8,128)(2,1)}, u32[]{:S(2)}) %copy-start) | copy-done | bytes 1966104
  3.8 0.0 copy-start.1
  3.8 1.1 %copy-done.1 = s32[128,1280]{1,0:T(8,128)S(1)} copy-done((s32[128,1280]{1,0:T(8,128)S(1)}, s32[128,1280]{1,0:T(8,128)}, u32[]{:S(2)}) %copy-start.1) | copy-done | bytes 655384
  4.9 63.6 %shard_map.68 = f32[8,4,1,256]{3,2,1,0:T(1,128)S(1)} custom-call(f32[2,16,128]{2,1,0:T(8,128)S(1)} %maximum_maximum_fusion.message_ref, bf16[768,1280]{1,0:T(8,128)(2,1)S(1)} %copy-done, s32[128,1280]{1,0:T(8,128)S(1)} %copy-done.1), custom_call_target="tpu_custom_call" | custom-call | tf_op jit(solution)/shard_map/pallas_call | solution.py:347
  68.5 0.1 slice.63
  68.6 0.1 copy.17
  68.7 0.1 copy.18
  68.8 0.1 reshape.53
  69.0 0.1 reshape.54
  69.2 0.6 dynamic-slice_reduce_fusion
  69.8 0.0 copy-done.2
  69.8 0.1 select_reduce_fusion.1
  70.0 0.1 broadcast_compare_fusion
  70.0 0.7 select_reduce_fusion
  (9 shorter events, 0.1 us)
Async XLA Ops:
  0.6 69.2 %copy-start.2 = (s32[16]{0:T(128)S(1)}, s32[16]{0:T(128)}, u32[]{:S(2)}) copy-start(s32[16]{0:T(128)} %param.9) | copy-start | bytes 196
  2.3 1.5 %copy-start = (bf16[768,1280]{1,0:T(8,128)(2,1)S(1)}, bf16[768,1280]{1,0:T(8,128)(2,1)}, u32[]{:S(2)}) copy-start(bf16[768,1280]{1,0:T(8,128)(2,1)} %dosage_ref.1) | copy-start | bytes 5898244
  3.8 1.1 %copy-start.1 = (s32[128,1280]{1,0:T(8,128)S(1)}, s32[128,1280]{1,0:T(8,128)}, u32[]{:S(2)}) copy-start(s32[128,1280]{1,0:T(8,128)} %perms_ref.1) | copy-start | bytes 1966084

commit v4 on v3

--- a/solution.py
+++ b/solution.py
@@ -80,6 +80,8 @@
     row_recv,
     all_send,
     all_recv,
+    shift_send,
+    shift_recv,
 ):
     var_dev, samp_dev = dosage_ref.shape
     permutations = perms_ref.shape[0]
@@ -158,7 +160,7 @@
                 ).wait_recv()
 
     alone[...] = jnp.zeros_like(alone)
-    sums = []
+    sums, codings = [], []
     for r in range(3):
         for pair in range(gene_dev // 2):
             codes = [[], []]
@@ -169,19 +171,25 @@
                 spread = whole_sum(sum(jnp.square(k - mean) for k in blocks)) / samples
                 factor = lax.rsqrt(spread + epsilon)
                 total = jnp.zeros((across, LANES), jnp.float32)
+                power = jnp.zeros((across, LANES), jnp.float32)
                 for k in range(samp_size):
                     value = ((blocks[k] - mean) * factor).astype(jnp.bfloat16).astype(jnp.float32)
                     total = total + value
-                    codes[half].append(encode(value))
+                    power = power + value * value
+                    if r == 1:
+                        codes[half].append(encode(value))
                 sums.append(whole_sum(total))
+                power = whole_sum(power) + 1e-30
+                inverse = lax.rsqrt(power)
+                codings.append((32000.0 * inverse, power * inverse / 32000.0))
                 own = (arrived[r, z, j, 0:across, :] - mean) * factor
                 own = own.astype(jnp.bfloat16).astype(jnp.float32)
                 row = r * gene_dev + j
                 for h in range(across):
                     alone[row : row + 1, h * LANES : (h + 1) * LANES] = own[h : h + 1, :]
-            word = r * (gene_dev // 2) + pair
-            for k in range(samp_size):
-                table[word, k, 0:across, :] = codes[0][k] + (codes[1][k] << 16)
+            if r == 1:
+                for k in range(samp_size):
+                    table[pair, k, 0:across, :] = codes[0][k] + (codes[1][k] << 16)
 
     each = alone[...].astype(jnp.bfloat16)
     for v in range(0, var_dev, step):
@@ -210,8 +218,10 @@
     power = powers()
     words = table.shape[0]
 
-    def block(target):
-        first = pl.multiple_of(target * share, share)
+    height = gene_dev * share
+
+    def gather(k):
+        first = pl.multiple_of(lax.rem(z + 1 + k, samp_size) * share, share)
 
         def tile(t, carry):
             p = pl.multiple_of((t // across) * 16, 16)
@@ -220,43 +230,91 @@
             low = index & (LANES - 1)
             high = index >> 7
             found = [jnp.zeros(index.shape, jnp.int32) for _ in range(words)]
-            for k in range(samp_size):
+            for c in range(samp_size):
                 for h in range(across):
-                    here = high == k * across + h
+                    here = high == c * across + h
                     for w in range(words):
-                        entry = jnp.broadcast_to(table[w, k, h : h + 1, :], index.shape)
+                        entry = jnp.broadcast_to(table[w, c, h : h + 1, :], index.shape)
                         found[w] = jnp.where(here, pick(entry, low), found[w])
             for w in range(words):
                 for half in range(2):
-                    row = pl.multiple_of((2 * w + half) * share + p, 16)
-                    shuffled[pl.ds(row, 16), pl.ds(s, LANES)] = decode(
+                    row = pl.multiple_of(height + (2 * w + half) * share + p, 16)
+                    shuffled[k, pl.ds(row, 16), pl.ds(s, LANES)] = decode(
                         found[w] >> (16 * half), power
                     )
             return carry
 
         lax.fori_loop(0, share // 16 * across, tile, 0)
-        taken = shuffled[...]
+
+    def shift(k, right):
+        side = 1 if right else 0
+        slot = 0 if right else 2
+        return send(
+            shuffled.at[k, pl.ds(height, height)],
+            shuffled.at[k, pl.ds(slot * height, height)],
+            shift_send.at[side, k],
+            shift_recv.at[side, k],
+            there(1 if right else -1, 0),
+        )
+
+    has_left, has_right = g > 0, g < gene_size - 1
+
+    def give(k):
+        pl.when(has_right)(lambda: shift(k, True).start())
+        pl.when(has_left)(lambda: shift(k, False).start())
+
+    def take(k):
+        pl.when(has_left)(lambda: shift(k, True).wait_recv())
+        pl.when(has_right)(lambda: shift(k, False).wait_recv())
+
+    def spent(k, carry):
+        pl.when(has_right)(lambda: shift(k, True).wait_send())
+        pl.when(has_left)(lambda: shift(k, False).wait_send())
+        return carry
+
+    def clear(slot):
+        for k in range(samp_size):
+            shuffled[k, slot * height : (slot + 1) * height, :] = jnp.zeros(
+                (height, samp_dev), jnp.bfloat16
+            )
+
+    pl.when(jnp.logical_not(has_left))(lambda: clear(0))
+    pl.when(jnp.logical_not(has_right))(lambda: clear(2))
+
+    def multiply(k):
+        take(k)
+        taken = shuffled[k]
         column = jnp.sum(taken.astype(jnp.float32), axis=1, keepdims=True)
         for v in range(0, var_dev, step):
-            mine[:, v : v + step] = (
+            centred = (
                 rows_dot(taken, dosage_ref[v : v + step, :]) - column * row_mean[:, v : v + step]
-            )
-
-    def remote(k, carry):
-        target = lax.rem(z + 1 + k, samp_size)
-        block(target)
-        outgoing[k] = mine[...].astype(jnp.bfloat16)
+            ) * row_scale[:, v : v + step]
+            for row in range(genes):
+                rows = slice(row * share, (row + 1) * share)
+                mine[rows, v : v + step] = centred[rows, :] * codings[row][0]
+
+    def remote(k):
+        multiply(k)
+        outgoing[k] = jnp.round(mine[...]).astype(jnp.int32).astype(jnp.int16)
         send(
             outgoing.at[k],
             incoming.at[k],
             block_send.at[k],
             block_recv.at[k],
-            {"gene": g, "samp": target},
+            {"gene": g, "samp": lax.rem(z + 1 + k, samp_size)},
         ).start()
+
+    gather(0)
+    give(0)
+
+    def turn(k, carry):
+        gather(k + 1)
+        give(k + 1)
+        remote(k)
         return carry
 
-    lax.fori_loop(0, samp_size - 1, remote, 0)
-    block(z)
+    lax.fori_loop(0, samp_size - 1, turn, 0)
+    multiply(samp_size - 1)
 
     for dz in range(1, samp_size):
         source = lax.rem(z + dz, samp_size)
@@ -285,12 +343,13 @@
         r, j = row // gene_dev, row % gene_dev
         start = arrived[r, 0, j, across : across + 1, 0:1]
         finish = arrived[r, 0, j, across + 1 : across + 2, 0:1]
-        weight = jnp.where((place >= start) & (place < finish), row_scale, 0.0)
+        inside = (place >= start) & (place < finish)
+        weight = jnp.where(inside, row_scale, 0.0)
         rows = slice(row * share, (row + 1) * share)
-        total = mine[rows, :] + row_mean * sums[row]
+        total = mine[rows, :] + row_mean * row_scale * (sums[row] * codings[row][0])
         for k in range(samp_size - 1):
-            total = total + incoming[k, rows, :].astype(jnp.float32)
-        peaks[rows, :] = fold(jnp.abs(total) * weight)
+            total = total + incoming[k, rows, :].astype(jnp.int32).astype(jnp.float32)
+        peaks[rows, :] = fold(jnp.where(inside, jnp.abs(total), 0.0)) * codings[row][1]
         last = genes * share + row
         peaks[last : last + 1, :] = fold(jnp.abs(direct[row : row + 1, :]) * weight)
     rows_z[z] = jnp.max(peaks[...].T, axis=0, keepdims=True)
@@ -315,6 +374,7 @@
         ).wait_recv()
     for copy in pending:
         copy.wait_send()
+    lax.fori_loop(0, samp_size, spent, 0)
 
 
 def up_to(size, unit):
@@ -351,21 +411,22 @@
         out_specs=pl.BlockSpec(memory_space=pltpu.VMEM),
         scratch_shapes=[
             pltpu.VMEM((3, samp_size, gene_dev, height, LANES), jnp.float32),
-            pltpu.VMEM((genes // 2, samp_size, up_to(across, 8), LANES), jnp.int32),
+            pltpu.VMEM((gene_dev // 2, samp_size, up_to(across, 8), LANES), jnp.int32),
             pltpu.VMEM((few, samp_dev), jnp.float32),
             pltpu.VMEM((samp_size, 16, var_dev), jnp.float32),
             pltpu.VMEM((samp_size, few, var_dev), jnp.float32),
-            pltpu.VMEM((genes * share, samp_dev), jnp.bfloat16),
+            pltpu.VMEM((samp_size, genes * share, samp_dev), jnp.bfloat16),
             pltpu.VMEM((genes * share, var_dev), jnp.float32),
-            pltpu.VMEM((samp_size - 1, genes * share, var_dev), jnp.bfloat16),
-            pltpu.VMEM((samp_size - 1, genes * share, var_dev), jnp.bfloat16),
+            pltpu.VMEM((samp_size - 1, genes * share, var_dev), jnp.int16),
+            pltpu.VMEM((samp_size - 1, genes * share, var_dev), jnp.int16),
             pltpu.VMEM((width, LANES), jnp.float32),
             pltpu.VMEM((samp_size, 1, width), jnp.float32),
             dma((3, samp_size)),
             dma((3, samp_size)),
         ]
         + [dma((samp_size,))] * 8
-        + [dma((gene_size,))] * 2,
+        + [dma((gene_size,))] * 2
+        + [dma((2, samp_size))] * 2,
         compiler_params=pltpu.CompilerParams(
             collective_id=0, has_side_effects=True, vmem_limit_bytes=48 * 2**20
         ),

time: 70.9 us -> 71.3 us (level)
  no operation moved by 1% of the time
where the time goes in v4:
time: 71.3 us; the launch traced here: 71 us
  Pallas kernels  64 us (90%)
  local copies, waits for them, and re-layouts  4.7 us (7%)
  other arithmetic  1.66 us (2%)
  between operations  0.73 us (1%)
    pallas_call x1, Pallas kernels, scan(): pl.pallas_call(kernel, out_shape=jax.ShapeDtypeStruct((gene_size, samp_si...  64 us
    unnamed x7, local copies, waits for them, and re-layouts  2.65 us

profile of v4, /device:TPU:0, one launch (start us, length us, event | category | flops | bytes accessed | tf_op | source)
XLA Modules:
  0.0 71.0 jit_solution(12225799743317467995)
XLA Ops:
  0.6 0.0 copy-start.2
  0.6 0.7 convert_element_type.3
  1.3 0.1 broadcast_in_dim.49
  1.4 0.7 %reshape.52 = f32[2,10,128]{2,1,0:T(8,128)S(1)} reshape(f32[2,1280]{1,0:T(2,128)} %bitcast.25) | data formatting | bytes 20480 | tf_op jit(solution)/shard_map/reshape | solution.py:395
  2.1 0.1 pad.8.clone
  2.2 0.1 maximum_maximum_fusion.message_ref
  2.3 0.0 copy-start
  2.3 1.5 %copy-done = bf16[768,1280]{1,0:T(8,128)(2,1)S(1)} copy-done((bf16[768,1280]{1,0:T(8,128)(2,1)S(1)}, bf16[768,1280]{1,0:T(8,128)(2,1)}, u32[]{:S(2)}) %copy-start) | copy-done | bytes 1966104
  3.8 0.0 copy-start.1
  3.8 1.1 %copy-done.1 = s32[128,1280]{1,0:T(8,128)S(1)} copy-done((s32[128,1280]{1,0:T(8,128)S(1)}, s32[128,1280]{1,0:T(8,128)}, u32[]{:S(2)}) %copy-start.1) | copy-done | bytes 655384
  4.9 64.0 %shard_map.68 = f32[8,4,1,256]{3,2,1,0:T(1,128)S(1)} custom-call(f32[2,16,128]{2,1,0:T(8,128)S(1)} %maximum_maximum_fusion.message_ref, bf16[768,1280]{1,0:T(8,128)(2,1)S(1)} %copy-done, s32[128,1280]{1,0:T(8,128)S(1)} %copy-done.1), custom_call_target="tpu_custom_call" | custom-call | tf_op jit(solution)/shard_map/pallas_call | solution.py:407
  68.9 0.1 slice.63
  69.0 0.1 copy.17
  69.1 0.1 copy.18
  69.2 0.1 reshape.53
  69.3 0.1 reshape.54
  69.6 0.6 dynamic-slice_reduce_fusion
  70.2 0.0 copy-done.2
  70.2 0.1 select_reduce_fusion.1
  70.3 0.1 broadcast_compare_fusion
  70.4 0.7 select_reduce_fusion
  (9 shorter events, 0.1 us)
Async XLA Ops:
  0.6 69.6 %copy-start.2 = (s32[16]{0:T(128)S(1)}, s32[16]{0:T(128)}, u32[]{:S(2)}) copy-start(s32[16]{0:T(128)} %param.9) | copy-start | bytes 196
  2.3 1.5 %copy-start = (bf16[768,1280]{1,0:T(8,128)(2,1)S(1)}, bf16[768,1280]{1,0:T(8,128)(2,1)}, u32[]{:S(2)}) copy-start(bf16[768,1280]{1,0:T(8,128)(2,1)} %dosage_ref.1) | copy-start | bytes 5898244
  3.8 1.1 %copy-start.1 = (s32[128,1280]{1,0:T(8,128)S(1)}, s32[128,1280]{1,0:T(8,128)}, u32[]{:S(2)}) copy-start(s32[128,1280]{1,0:T(8,128)} %perms_ref.1) | copy-start | bytes 1966084

commit v5 on v4

--- a/solution.py
+++ b/solution.py
@@ -227,15 +227,19 @@
             p = pl.multiple_of((t // across) * 16, 16)
             s = pl.multiple_of((t % across) * LANES, LANES)
             index = perms_ref[pl.ds(pl.multiple_of(first + p, 16), 16), pl.ds(s, LANES)]
-            low = index & (LANES - 1)
-            high = index >> 7
-            found = [jnp.zeros(index.shape, jnp.int32) for _ in range(words)]
-            for c in range(samp_size):
-                for h in range(across):
-                    here = high == c * across + h
-                    for w in range(words):
-                        entry = jnp.broadcast_to(table[w, c, h : h + 1, :], index.shape)
-                        found[w] = jnp.where(here, pick(entry, low), found[w])
+            parts = []
+            for part in (index[0:8], index[8:16]):
+                low = part & (LANES - 1)
+                high = part >> 7
+                picked = [jnp.zeros(part.shape, jnp.int32) for _ in range(words)]
+                for c in range(samp_size):
+                    for h in range(across):
+                        here = high == c * across + h
+                        for w in range(words):
+                            entry = jnp.broadcast_to(table[w, c, h : h + 1, :], part.shape)
+                            picked[w] = jnp.where(here, pick(entry, low), picked[w])
+                parts.append(picked)
+            found = [jnp.concatenate(pair, axis=0) for pair in zip(*parts)]
             for w in range(words):
                 for half in range(2):
                     row = pl.multiple_of(height + (2 * w + half) * share + p, 16)

time: 71.3 us -> 71.4 us (level)
  no operation moved by 1% of the time
where the time goes in v5:
time: 71.4 us; the launch traced here: 71.2 us
  Pallas kernels  64.1 us (90%)
  local copies, waits for them, and re-layouts  4.7 us (7%)
  other arithmetic  1.66 us (2%)
  between operations  0.73 us (1%)
    pallas_call x1, Pallas kernels, scan(): pl.pallas_call(kernel, out_shape=jax.ShapeDtypeStruct((gene_size, samp_si...  64.1 us
    unnamed x7, local copies, waits for them, and re-layouts  2.65 us

profile of v5, /device:TPU:0, one launch (start us, length us, event | category | flops | bytes accessed | tf_op | source)
XLA Modules:
  0.0 71.2 jit_solution(8946865397509211437)
XLA Ops:
  0.6 0.0 copy-start.2
  0.6 0.7 convert_element_type.3
  1.3 0.1 broadcast_in_dim.49
  1.4 0.7 %reshape.52 = f32[2,10,128]{2,1,0:T(8,128)S(1)} reshape(f32[2,1280]{1,0:T(2,128)} %bitcast.25) | data formatting | bytes 20480 | tf_op jit(solution)/shard_map/reshape | solution.py:399
  2.1 0.1 pad.8.clone
  2.2 0.1 maximum_maximum_fusion.message_ref
  2.3 0.0 copy-start
  2.3 1.5 %copy-done = bf16[768,1280]{1,0:T(8,128)(2,1)S(1)} copy-done((bf16[768,1280]{1,0:T(8,128)(2,1)S(1)}, bf16[768,1280]{1,0:T(8,128)(2,1)}, u32[]{:S(2)}) %copy-start) | copy-done | bytes 1966104
  3.8 0.0 copy-start.1
  3.8 1.1 %copy-done.1 = s32[128,1280]{1,0:T(8,128)S(1)} copy-done((s32[128,1280]{1,0:T(8,128)S(1)}, s32[128,1280]{1,0:T(8,128)}, u32[]{:S(2)}) %copy-start.1) | copy-done | bytes 655384
  4.9 64.1 %shard_map.68 = f32[8,4,1,256]{3,2,1,0:T(1,128)S(1)} custom-call(f32[2,16,128]{2,1,0:T(8,128)S(1)} %maximum_maximum_fusion.message_ref, bf16[768,1280]{1,0:T(8,128)(2,1)S(1)} %copy-done, s32[128,1280]{1,0:T(8,128)S(1)} %copy-done.1), custom_call_target="tpu_custom_call" | custom-call | tf_op jit(solution)/shard_map/pallas_call | solution.py:411
  69.0 0.1 slice.63
  69.1 0.1 copy.17
  69.2 0.1 copy.18
  69.3 0.1 reshape.53
  69.5 0.1 reshape.54
  69.7 0.6 dynamic-slice_reduce_fusion
  70.3 0.0 copy-done.2
  70.3 0.1 select_reduce_fusion.1
  70.5 0.1 broadcast_compare_fusion
  70.5 0.7 select_reduce_fusion
  (9 shorter events, 0.1 us)
Async XLA Ops:
  0.6 69.7 %copy-start.2 = (s32[16]{0:T(128)S(1)}, s32[16]{0:T(128)}, u32[]{:S(2)}) copy-start(s32[16]{0:T(128)} %param.9) | copy-start | bytes 196
  2.3 1.5 %copy-start = (bf16[768,1280]{1,0:T(8,128)(2,1)S(1)}, bf16[768,1280]{1,0:T(8,128)(2,1)}, u32[]{:S(2)}) copy-start(bf16[768,1280]{1,0:T(8,128)(2,1)} %dosage_ref.1) | copy-start | bytes 5898244
  3.8 1.1 %copy-start.1 = (s32[128,1280]{1,0:T(8,128)S(1)}, s32[128,1280]{1,0:T(8,128)}, u32[]{:S(2)}) copy-start(s32[128,1280]{1,0:T(8,128)} %perms_ref.1) | copy-start | bytes 1966084

commit v6 on v5

--- a/solution.py
+++ b/solution.py
@@ -80,8 +80,6 @@
     row_recv,
     all_send,
     all_recv,
-    shift_send,
-    shift_recv,
 ):
     var_dev, samp_dev = dosage_ref.shape
     permutations = perms_ref.shape[0]
@@ -176,8 +174,7 @@
                     value = ((blocks[k] - mean) * factor).astype(jnp.bfloat16).astype(jnp.float32)
                     total = total + value
                     power = power + value * value
-                    if r == 1:
-                        codes[half].append(encode(value))
+                    codes[half].append(encode(value))
                 sums.append(whole_sum(total))
                 power = whole_sum(power) + 1e-30
                 inverse = lax.rsqrt(power)
@@ -187,9 +184,9 @@
                 row = r * gene_dev + j
                 for h in range(across):
                     alone[row : row + 1, h * LANES : (h + 1) * LANES] = own[h : h + 1, :]
-            if r == 1:
-                for k in range(samp_size):
-                    table[pair, k, 0:across, :] = codes[0][k] + (codes[1][k] << 16)
+            word = r * (gene_dev // 2) + pair
+            for k in range(samp_size):
+                table[word, k, 0:across, :] = codes[0][k] + (codes[1][k] << 16)
 
     each = alone[...].astype(jnp.bfloat16)
     for v in range(0, var_dev, step):
@@ -217,8 +214,6 @@
 
     power = powers()
     words = table.shape[0]
-
-    height = gene_dev * share
 
     def gather(k):
         first = pl.multiple_of(lax.rem(z + 1 + k, samp_size) * share, share)
@@ -242,7 +237,7 @@
             found = [jnp.concatenate(pair, axis=0) for pair in zip(*parts)]
             for w in range(words):
                 for half in range(2):
-                    row = pl.multiple_of(height + (2 * w + half) * share + p, 16)
+                    row = pl.multiple_of((2 * w + half) * share + p, 16)
                     shuffled[k, pl.ds(row, 16), pl.ds(s, LANES)] = decode(
                         found[w] >> (16 * half), power
                     )
@@ -250,43 +245,7 @@
 
         lax.fori_loop(0, share // 16 * across, tile, 0)
 
-    def shift(k, right):
-        side = 1 if right else 0
-        slot = 0 if right else 2
-        return send(
-            shuffled.at[k, pl.ds(height, height)],
-            shuffled.at[k, pl.ds(slot * height, height)],
-            shift_send.at[side, k],
-            shift_recv.at[side, k],
-            there(1 if right else -1, 0),
-        )
-
-    has_left, has_right = g > 0, g < gene_size - 1
-
-    def give(k):
-        pl.when(has_right)(lambda: shift(k, True).start())
-        pl.when(has_left)(lambda: shift(k, False).start())
-
-    def take(k):
-        pl.when(has_left)(lambda: shift(k, True).wait_recv())
-        pl.when(has_right)(lambda: shift(k, False).wait_recv())
-
-    def spent(k, carry):
-        pl.when(has_right)(lambda: shift(k, True).wait_send())
-        pl.when(has_left)(lambda: shift(k, False).wait_send())
-        return carry
-
-    def clear(slot):
-        for k in range(samp_size):
-            shuffled[k, slot * height : (slot + 1) * height, :] = jnp.zeros(
-                (height, samp_dev), jnp.bfloat16
-            )
-
-    pl.when(jnp.logical_not(has_left))(lambda: clear(0))
-    pl.when(jnp.logical_not(has_right))(lambda: clear(2))
-
     def multiply(k):
-        take(k)
         taken = shuffled[k]
         column = jnp.sum(taken.astype(jnp.float32), axis=1, keepdims=True)
         for v in range(0, var_dev, step):
@@ -308,16 +267,13 @@
             {"gene": g, "samp": lax.rem(z + 1 + k, samp_size)},
         ).start()
 
-    gather(0)
-    give(0)
-
     def turn(k, carry):
-        gather(k + 1)
-        give(k + 1)
+        gather(k)
         remote(k)
         return carry
 
     lax.fori_loop(0, samp_size - 1, turn, 0)
+    gather(samp_size - 1)
     multiply(samp_size - 1)
 
     for dz in range(1, samp_size):
@@ -378,7 +334,6 @@
         ).wait_recv()
     for copy in pending:
         copy.wait_send()
-    lax.fori_loop(0, samp_size, spent, 0)
 
 
 def up_to(size, unit):
@@ -415,7 +370,7 @@
         out_specs=pl.BlockSpec(memory_space=pltpu.VMEM),
         scratch_shapes=[
             pltpu.VMEM((3, samp_size, gene_dev, height, LANES), jnp.float32),
-            pltpu.VMEM((gene_dev // 2, samp_size, up_to(across, 8), LANES), jnp.int32),
+            pltpu.VMEM((genes // 2, samp_size, up_to(across, 8), LANES), jnp.int32),
             pltpu.VMEM((few, samp_dev), jnp.float32),
             pltpu.VMEM((samp_size, 16, var_dev), jnp.float32),
             pltpu.VMEM((samp_size, few, var_dev), jnp.float32),
@@ -429,8 +384,7 @@
             dma((3, samp_size)),
         ]
         + [dma((samp_size,))] * 8
-        + [dma((gene_size,))] * 2
-        + [dma((2, samp_size))] * 2,
+        + [dma((gene_size,))] * 2,
         compiler_params=pltpu.CompilerParams(
             collective_id=0, has_side_effects=True, vmem_limit_bytes=48 * 2**20
         ),

time: 71.4 us -> 70.9 us (level)
  no operation moved by 1% of the time
where the time goes in v6:
time: 70.9 us; the launch traced here: 70.7 us
  Pallas kernels  63.6 us (90%)
  local copies, waits for them, and re-layouts  4.7 us (7%)
  other arithmetic  1.66 us (2%)
  between operations  0.73 us (1%)
    pallas_call x1, Pallas kernels, scan(): pl.pallas_call(kernel, out_shape=jax.ShapeDtypeStruct((gene_size, samp_si...  63.6 us
    unnamed x7, local copies, waits for them, and re-layouts  2.65 us

profile of v6, /device:TPU:0, one launch (start us, length us, event | category | flops | bytes accessed | tf_op | source)
XLA Modules:
  0.0 70.7 jit_solution(10018422597466972007)
XLA Ops:
  0.6 0.0 copy-start.2
  0.6 0.7 convert_element_type.3
  1.3 0.1 broadcast_in_dim.49
  1.4 0.7 %reshape.52 = f32[2,10,128]{2,1,0:T(8,128)S(1)} reshape(f32[2,1280]{1,0:T(2,128)} %bitcast.25) | data formatting | bytes 20480 | tf_op jit(solution)/shard_map/reshape | solution.py:354
  2.1 0.1 pad.8.clone
  2.2 0.1 maximum_maximum_fusion.message_ref
  2.3 0.0 copy-start
  2.3 1.5 %copy-done = bf16[768,1280]{1,0:T(8,128)(2,1)S(1)} copy-done((bf16[768,1280]{1,0:T(8,128)(2,1)S(1)}, bf16[768,1280]{1,0:T(8,128)(2,1)}, u32[]{:S(2)}) %copy-start) | copy-done | bytes 1966104
  3.8 0.0 copy-start.1
  3.8 1.1 %copy-done.1 = s32[128,1280]{1,0:T(8,128)S(1)} copy-done((s32[128,1280]{1,0:T(8,128)S(1)}, s32[128,1280]{1,0:T(8,128)}, u32[]{:S(2)}) %copy-start.1) | copy-done | bytes 655384
  4.9 63.6 %shard_map.68 = f32[8,4,1,256]{3,2,1,0:T(1,128)S(1)} custom-call(f32[2,16,128]{2,1,0:T(8,128)S(1)} %maximum_maximum_fusion.message_ref, bf16[768,1280]{1,0:T(8,128)(2,1)S(1)} %copy-done, s32[128,1280]{1,0:T(8,128)S(1)} %copy-done.1), custom_call_target="tpu_custom_call" | custom-call | tf_op jit(solution)/shard_map/pallas_call | solution.py:366
  68.5 0.1 slice.63
  68.6 0.1 copy.17
  68.7 0.1 copy.18
  68.8 0.1 reshape.53
  69.0 0.1 reshape.54
  69.2 0.6 dynamic-slice_reduce_fusion
  69.8 0.0 copy-done.2
  69.8 0.1 select_reduce_fusion.1
  69.9 0.1 broadcast_compare_fusion
  70.0 0.7 select_reduce_fusion
  (9 shorter events, 0.1 us)
Async XLA Ops:
  0.6 69.2 %copy-start.2 = (s32[16]{0:T(128)S(1)}, s32[16]{0:T(128)}, u32[]{:S(2)}) copy-start(s32[16]{0:T(128)} %param.9) | copy-start | bytes 196
  2.3 1.5 %copy-start = (bf16[768,1280]{1,0:T(8,128)(2,1)S(1)}, bf16[768,1280]{1,0:T(8,128)(2,1)}, u32[]{:S(2)}) copy-start(bf16[768,1280]{1,0:T(8,128)(2,1)} %dosage_ref.1) | copy-start | bytes 5898244
  3.8 1.1 %copy-start.1 = (s32[128,1280]{1,0:T(8,128)S(1)}, s32[128,1280]{1,0:T(8,128)}, u32[]{:S(2)}) copy-start(s32[128,1280]{1,0:T(8,128)} %perms_ref.1) | copy-start | bytes 1966084
